TPU v7x, 256 devices: a whole 4x4x8 slice. The times are simulated.
256 devices in a mesh: chord: 8 (over y, x_lo), span: 32 (over x_hi, z, core).
Axes of the slice: x: 4 (x_hi: 2, x_lo: 2; x = x_hi * 2 + x_lo), y: 4, z: 8, core: 2. Of those that a mesh axis runs over, the one named last changes fastest.
Arguments:
- velocity: float32 [3, 8, 256, 8192], P(None, None, 'chord', 'span'), may hold values from -6 to 6
- stress: float32 [6, 8, 256, 8192], P(None, None, 'chord', 'span'), may hold values from -6 to 6
- material: int32 [8, 256, 8192], P(None, 'chord', 'span'), may hold values from 0 to 3
- moduli: float32 [4, 10], replicated, may hold values from 0.2 to 0.8
- drive: float32 [1024, 128], P(('chord', 'span')), may hold values from -6 to 6
- owner: int32 [1024, 1], replicated, may hold values from 0 to 255; in each aligned block of 1024 rows (0 to 1023, 1024 to 2047, ...) at most 16 rows name the same one
- cells: int32 [1024, 64], replicated, may hold values from 0 to 8191, as said below
Outputs:
- velocity_out: float32 [3, 8, 256, 8192], P(None, None, 'chord', 'span')
- stress_out: float32 [6, 8, 256, 8192], P(None, None, 'chord', 'span')
- records: float32 [1024, 128], P(('chord', 'span'))
Inputs may be any that keep to these rules, and one draw needn't show every extreme that they name: `owner`: every device owns at least one patch and none owns more than 16; some device owns exactly 16. The cells of one patch form a square of 8 x 8 cells inside its owner's tile; cell q lies q // 8 rows and q % 8 columns from cell 0.
All inputs are finite; a program needn't handle non-finite values.
Results may differ from a plain program's by a relative error of at most 0.0001.
Values sent between devices are 32-bit elements; how exact they have to be, the bound alone decides.
A program may use at most 64 MiB of HBM per device.

v0:
```python
import functools

import jax
import jax.numpy as jnp
from jax import lax
from jax.experimental import pallas as pl
from jax.experimental.pallas import tpu as pltpu
from jax.sharding import PartitionSpec as P

MESH = pl.DeviceIdType.MESH
F32 = jnp.float32
BF16 = jnp.bfloat16
DT = 0.5
SLOTS = 16
PATCH = 8
LANES = 128
SPLIT_X_HI, SPLIT_Z, SPLIT_CORE = 2, 8, 2
C11, C12, C13, C22, C23, C33, C44, C55, C66, BUOY = range(10)
XX, YY, ZZ, YZ, XZ, XY = range(6)


def iota(shape, dim):
    return lax.broadcasted_iota(jnp.int32, shape, dim)


def fiota(shape, dim):
    return iota(shape, dim).astype(F32)


def split(x):
    a = x.astype(BF16)
    return a, (x - a.astype(F32)).astype(BF16)


def dot(a, b, contract=((1,), (0,))):
    return lax.dot_general(a, b, (contract, ((), ())), preferred_element_type=F32)


def kernel(
    n_chord,
    n_span,
    vel_in,
    str_in,
    mat_in,
    moduli_in,
    drive_in,
    owner_in,
    cells_in,
    v,
    s,
    rec_out,
    mat,
    moduli,
    drive,
    owner,
    cells,
    coef,
    onehot_y,
    slot_x,
    slot_y,
    plane,
    ranks,
    taken,
    taken_t,
    gathered,
    send2,
    routed2,
    send3,
    routed3,
    rec_send,
    rec_rows,
    rec_back,
    rec_got,
    to_dn,
    to_up,
    to_rt,
    to_lt,
    from_up,
    from_dn,
    from_lt,
    from_rt,
    corner_up,
    corner_dn,
    vto_dn,
    vto_up,
    vto_rt,
    vto_lt,
    vfrom_up,
    vfrom_dn,
    vfrom_lt,
    vfrom_rt,
    vcorner_up,
    vcorner_dn,
    aux_t,
    off_y,
    off_x,
    edge_pick,
    halo_row,
    halo_col,
    hcoef_row,
    hcoef_col,
    load_sem,
    group_send,
    group_recv,
    edge_send,
    edge_recv,
):
    c = lax.axis_index("chord")
    sp = lax.axis_index("span")
    depth = vel_in.shape[1]
    size_x = vel_in.shape[2]
    size_y = vel_in.shape[3]
    half = size_y - LANES
    n_z = SPLIT_Z
    n_p = n_chord * SPLIT_X_HI * SPLIT_CORE
    my_z = lax.rem(lax.div(sp, SPLIT_CORE), SPLIT_Z)
    x_hi = lax.div(sp, SPLIT_Z * SPLIT_CORE)
    my_p = (c * SPLIT_X_HI + x_hi) * SPLIT_CORE + lax.rem(sp, SPLIT_CORE)
    xor = jnp.bitwise_xor

    def p_partner(i):
        core, high, to_c = i % SPLIT_CORE, i // SPLIT_CORE % SPLIT_X_HI, i // SPLIT_CORE // SPLIT_X_HI
        return xor(c, to_c), xor(sp, high * SPLIT_Z * SPLIT_CORE + core)

    def z_partner(i):
        return c, xor(sp, i * SPLIT_CORE)

    has_up, has_dn = c > 0, c < n_chord - 1
    has_lt, has_rt = sp > 0, sp < n_span - 1
    diag_up = jnp.logical_and(has_up, has_rt)
    diag_dn = jnp.logical_and(has_dn, has_lt)

    pairs = [
        (drive_in, drive),
        (vel_in, v),
        (str_in, s),
        (mat_in, mat),
        (owner_in, owner),
        (cells_in.at[pl.ds(0, 8)], cells),
        (moduli_in, moduli),
    ]
    loads = [pltpu.make_async_copy(a, b, load_sem.at[i]) for i, (a, b) in enumerate(pairs)]
    loads[0].start()

    barrier = pltpu.get_barrier_semaphore()

    def greet(to_c, to_s):
        pl.semaphore_signal(barrier, inc=1, device_id=(to_c, to_s), device_id_type=MESH)

    ring = (0, 1, 2, 1)

    def p_hops(i):
        core, high, to_c = i % SPLIT_CORE, i // SPLIT_CORE % SPLIT_X_HI, i // SPLIT_CORE // SPLIT_X_HI
        return 4 * (ring[2 * high + to_c % 2] + ring[to_c // 2 % 4]) + core

    p_order = sorted(range(1, n_p), key=p_hops, reverse=True)
    z_order = sorted(range(1, n_z), key=lambda i: (0, 1, 2, 3, 4, 3, 2, 3)[i], reverse=True)
    for i in p_order:
        greet(*p_partner(i))
    for i in z_order:
        greet(*z_partner(i))
    sides = [
        (has_up, (c - 1, sp)),
        (has_dn, (c + 1, sp)),
        (has_lt, (c, sp - 1)),
        (has_rt, (c, sp + 1)),
        (diag_up, (c - 1, sp + 1)),
        (diag_dn, (c + 1, sp - 1)),
    ]
    for there, to in sides:
        pl.when(there)(functools.partial(greet, *to))
    for load in loads[1:]:
        load.start()

    @pl.when(jnp.logical_not(has_up))
    def _():
        for ref in (from_up, vfrom_up):
            ref[...] = jnp.zeros_like(ref)

    @pl.when(jnp.logical_not(has_dn))
    def _():
        for ref in (from_dn, vfrom_dn):
            ref[...] = jnp.zeros_like(ref)

    @pl.when(jnp.logical_not(has_lt))
    def _():
        for ref in (from_lt, vfrom_lt):
            ref[...] = jnp.zeros_like(ref)

    @pl.when(jnp.logical_not(has_rt))
    def _():
        for ref in (from_rt, vfrom_rt):
            ref[...] = jnp.zeros_like(ref)

    @pl.when(jnp.logical_not(diag_up))
    def _():
        for ref in (corner_up, vcorner_up):
            ref[...] = jnp.zeros_like(ref)

    @pl.when(jnp.logical_not(diag_dn))
    def _():
        for ref in (corner_dn, vcorner_dn):
            ref[...] = jnp.zeros_like(ref)

    pl.semaphore_wait(
        barrier,
        n_p + n_z - 2 + sum(there.astype(jnp.int32) for there, _ in sides),
    )

    def send(source, target, to, sem):
        return pltpu.make_async_remote_copy(
            src_ref=source,
            dst_ref=target,
            send_sem=group_send.at[sem],
            recv_sem=group_recv.at[sem],
            device_id=to,
            device_id_type=MESH,
        )

    def wait_all(ref, count, sems, sem):
        if count:
            part = ref.at[pl.ds(0, count)]
            pltpu.make_async_copy(part, part, sems.at[sem]).wait()

    def block(ref, index, count):
        return ref.at[pl.ds(pl.multiple_of(index * count, count), count)]

    per = drive.shape[0]
    loads[0].wait()
    for i in p_order:
        send(drive, block(gathered, my_p, per), p_partner(i), 0).start()
    gathered[pl.ds(pl.multiple_of(my_p * per, per), per), :] = drive[...]

    def edge(source, target, to, index):
        return pltpu.make_async_remote_copy(
            src_ref=source,
            dst_ref=target,
            send_sem=edge_send.at[index],
            recv_sem=edge_recv.at[index],
            device_id=to,
            device_id_type=MESH,
        )

    up, dn, lt, rt = (c - 1, sp), (c + 1, sp), (c, sp - 1), (c, sp + 1)

    def exchange(first, up_src, dn_src, lt_src, rt_src, up_dst, dn_dst, lt_dst, rt_dst, corners):
        moves = [
            (has_up, has_dn, edge(up_src, dn_dst, up, first)),
            (has_dn, has_up, edge(dn_src, up_dst, dn, first + 1)),
            (has_lt, has_rt, edge(lt_src, rt_dst, lt, first + 2)),
            (has_rt, has_lt, edge(rt_src, lt_dst, rt, first + 3)),
        ]
        corner_from_dn, corner_from_up = corners
        vy_corner = up_src.at[pl.ds(depth, depth), pl.ds(half, LANES)]
        vx_corner = dn_src.at[pl.ds(0, depth), pl.ds(0, LANES)]
        moves += [
            (diag_up, diag_dn, edge(vy_corner, corner_from_dn, (c - 1, sp + 1), first + 4)),
            (diag_dn, diag_up, edge(vx_corner, corner_from_up, (c + 1, sp - 1), first + 5)),
        ]

        def start():
            for goes, _, copy in moves:
                pl.when(goes)(copy.start)

        def arrive():
            for _, comes, copy in moves:
                pl.when(comes)(copy.wait_recv)

        def leave():
            for goes, _, copy in moves:
                pl.when(goes)(copy.wait_send)

        return start, arrive, leave

    start1, arrive1, leave1 = exchange(
        0, to_up, to_dn, to_lt, to_rt, from_up, from_dn, from_lt, from_rt, (corner_dn, corner_up)
    )
    start2, arrive2, leave2 = exchange(
        6, vto_up, vto_dn, vto_lt, vto_rt, vfrom_up, vfrom_dn, vfrom_lt, vfrom_rt, (vcorner_dn, vcorner_up)
    )

    def pack_rows(ref, row, fields):
        for z in range(depth):
            for k, read in enumerate(fields):
                ref[k * depth + z : k * depth + z + 1, :] = read(z, row)

    lane = iota((size_x, LANES), 1)
    row = iota((size_x, size_y), 0)

    def pack_cols(ref, column, fields):
        base = 0 if column == 0 else half
        at = column - base

        acc = jnp.zeros((size_x, LANES), F32)
        for z in range(depth):
            for k, read in enumerate(fields):
                to = k * depth + z
                by = (to + LANES - at) % LANES
                tile = read(z, base)
                moved = pltpu.roll(tile, by, 1) if by else tile
                acc = jnp.where(lane == to, moved, acc)
        ref[...] = acc

    def row_of(ref, comp):
        return lambda z, r: ref[comp, z, r : r + 1, :]

    def col_of(ref, comp):
        return lambda z, base: ref[comp, z, :, base : base + LANES]

    def mat_row(z, r):
        return mat[z, r : r + 1, :].astype(F32)

    def mat_col(z, base):
        return mat[z, :, base : base + LANES].astype(F32)

    v_rows = [row_of(v, k) for k in range(3)]
    v_cols = [col_of(v, k) for k in range(3)]

    for load in loads[1:]:
        load.wait()
    pack_rows(to_dn, size_x - 1, v_rows + [row_of(s, XY), row_of(s, XZ), mat_row])
    pack_rows(to_up, 0, v_rows + [row_of(s, XX), mat_row])
    pack_cols(to_rt, size_y - 1, v_cols + [col_of(s, XY), col_of(s, YZ), mat_col])
    pack_cols(to_lt, 0, v_cols + [col_of(s, YY), mat_col])
    start1()

    n_block = owner.shape[0]
    earlier = (iota((LANES, LANES), 0) < iota((LANES, LANES), 1)).astype(BF16)
    ones = jnp.ones((LANES, LANES), BF16)
    wanted = c * n_span + sp + (iota((n_z, LANES), 0) - my_z) * SPLIT_CORE
    same = jnp.concatenate(
        [(owner[a : a + 1, :] == wanted).astype(F32) for a in range(n_block)], axis=0
    )
    counts = dot(same.astype(BF16), jnp.concatenate([earlier, ones], axis=1))
    before = jnp.zeros((n_z, LANES), F32)
    chunk = SPLIT_CORE * per
    rank = jnp.full((n_z, LANES), -1.0, F32)
    lane8 = iota((n_z, LANES), 1)
    shift = size_y.bit_length() - 1
    aux = jnp.zeros((8, LANES), F32)
    aux_lane, aux_row = iota((8, LANES), 1), iota((8, LANES), 0)
    for a in range(n_block):
        at = slice(a * n_z, (a + 1) * n_z)
        rank_a = jnp.where(same[at] > 0.5, before + counts[at, :LANES], -1.0)
        before = before + counts[at, LANES:]
        ranks[at, :] = rank_a
        anchor = cells[0:1, a * LANES : (a + 1) * LANES]
        fields = (owner[a : a + 1, :], anchor >> shift, anchor & (size_y - 1))
        aux_a = jnp.zeros((8, LANES), F32)
        for k, field in enumerate(fields):
            aux_a = jnp.where(aux_row == k, field.astype(F32), aux_a)
        for h in range(SPLIT_X_HI):
            to = (a * SPLIT_X_HI + h) * chunk
            by = (to - h * SPLIT_Z * chunk) % LANES + LANES - my_z * chunk
            moved = pltpu.roll(rank_a, lax.rem(by, LANES), 1)
            rank = jnp.where(jnp.logical_and(lane8 >= to, lane8 < to + chunk), moved, rank)
            moved = pltpu.roll(aux_a, lax.rem(by, LANES), 1)
            aux = jnp.where(jnp.logical_and(aux_lane >= to, aux_lane < to + chunk), moved, aux)
    slot_ids = fiota((SLOTS, LANES), 0)
    for h in range(2):
        for k in range(n_z):
            at = (h * n_z + k) * 8
            ids = slot_ids[h * 8 : (h + 1) * 8]
            taken[at : at + 8, :] = (rank[k : k + 1, :] == ids).astype(F32)
    side_row = iota((n_z * 8, LANES), 0)
    side = side_row & 7
    to_z = side_row >> 3
    to_span = sp + (to_z - my_z) * SPLIT_CORE
    is_dn = jnp.logical_and((side & 1) == 0, side < 4)
    is_up = jnp.logical_and((side & 1) == 1, side < 4)
    is_rt = jnp.logical_and(side == 4, to_span < n_span - 1)
    is_lt = jnp.logical_and(side == 5, to_span > 0)
    whose = (c * n_span + to_span).astype(F32)
    at_owner, at_x, at_y = aux[0:1, :], aux[1:2, :], aux[2:3, :]
    reach = PATCH - 1
    edge_pick[...] = jnp.where(
        is_dn,
        jnp.logical_and(at_owner == whose + n_span, at_x == 0).astype(F32),
        jnp.where(
            is_up,
            jnp.logical_and(at_owner == whose - n_span, at_x == size_x - 1 - reach).astype(F32),
            jnp.where(
                is_rt,
                jnp.logical_and(at_owner == whose + 1, at_y == 0).astype(F32),
                jnp.where(
                    is_lt,
                    jnp.logical_and(at_owner == whose - 1, at_y == size_y - 1 - reach).astype(F32),
                    0.0,
                ),
            ),
        ),
    )
    aux_t[...] = jnp.transpose(jnp.concatenate([aux, jnp.zeros((LANES - 8, LANES), F32)], axis=0))
    off_x[...] = iota((LANES, LANES), 1) - aux_t[:, 1:2].astype(jnp.int32)
    off_y[...] = iota((LANES, size_y), 1) - aux_t[:, 2:3].astype(jnp.int32)

    taken_t[...] = jnp.transpose(taken[...])
    first_x = jnp.zeros((SLOTS, LANES), F32)
    first_y = jnp.zeros((SLOTS, LANES), F32)
    for a in range(n_block):
        anchor = cells[0:1, a * LANES : (a + 1) * LANES]
        hit = ranks[pl.ds(a * n_z + my_z, 1), :] == slot_ids
        first_x = first_x + jnp.where(hit, (anchor >> shift).astype(F32), 0.0)
        first_y = first_y + jnp.where(hit, (anchor & (size_y - 1)).astype(F32), 0.0)
    first_x = jnp.sum(first_x, axis=1, keepdims=True)
    first_y = jnp.sum(first_y, axis=1, keepdims=True)
    low = iota((8, LANES), 1) < 64
    cell_id = iota((8, LANES), 1) & 63
    slot_x[...] = jnp.where(low, first_x[0:8], first_x[8:16]) + (cell_id >> 3).astype(F32)
    slot_y[...] = jnp.where(low, first_y[0:8], first_y[8:16]) + (cell_id & 7).astype(F32)
    y_ids = fiota((size_y, LANES), 0)
    for t in range(8):
        onehot_y[:, t * LANES : (t + 1) * LANES] = (
            (slot_y[t : t + 1, :] == y_ids).astype(F32).astype(BF16)
        )
    x_ids = fiota((size_x, LANES), 0)

    def table(kind, index):
        out = jnp.full(kind.shape, DT * moduli[0, index], F32)
        for m in range(1, 4):
            out = jnp.where(kind == m, DT * moduli[m, index], out)
        return out

    def coef_layer(z, _):
        kind = mat[z]
        for k in range(10):
            coef[k, z] = table(kind, k)
        return 0

    lax.fori_loop(0, depth, coef_layer, 0)

    def along_x(field, by, edge_row):
        if by > 0:
            return jnp.where(row == 0, edge_row, pltpu.roll(field, 1, 0))
        return jnp.where(row == size_x - 1, edge_row, pltpu.roll(field, size_x - 1, 0))

    def along_y(field, by, edge_col):
        if by > 0:
            moved = pltpu.roll(field, 1, 1)
            head = jnp.where(lane == 0, edge_col, moved[:, :LANES])
            return jnp.concatenate([head, moved[:, LANES:]], axis=1)
        moved = pltpu.roll(field, size_y - 1, 1)
        tail = jnp.where(lane == LANES - 1, edge_col, moved[:, half:])
        return jnp.concatenate([moved[:, :half], tail], axis=1)

    def first_lane(ref, field, z):
        return pltpu.roll(ref[...], lax.rem(2 * LANES - (field * depth + z), LANES), 1)

    def last_lane(ref, field, z):
        return pltpu.roll(ref[...], lax.rem(2 * LANES - 1 - (field * depth + z), LANES), 1)

    bottom, top = 0, depth - 1

    def stress_layer(z, up_ref, dn_ref, lt_ref, rt_ref):
        is_bottom, is_top = isinstance(z, int) and z == bottom, isinstance(z, int) and z == top
        vx, vy, vz = v[0, z], v[1, z], v[2, z]
        zz = vz if is_bottom else vz - v[2, z - 1]
        zy = -vy if is_top else v[1, z + 1] - vy
        zx = -vx if is_top else v[0, z + 1] - vx
        if up_ref is None:
            vx_up = vy_dn = vz_dn = vy_lt = vx_rt = vz_rt = 0.0
        else:
            vx_up = up_ref[pl.ds(z, 1), :]
            vy_dn, vz_dn = dn_ref[pl.ds(depth + z, 1), :], dn_ref[pl.ds(2 * depth + z, 1), :]
            vy_lt = first_lane(lt_ref, 1, z)
            vx_rt, vz_rt = last_lane(rt_ref, 0, z), last_lane(rt_ref, 2, z)
        xx = vx - along_x(vx, 1, vx_up)
        yy = vy - along_y(vy, 1, vy_lt)
        yz = zy + (along_y(vz, -1, vz_rt) - vz)
        xz = zx + (along_x(vz, -1, vz_dn) - vz)
        xy = (along_y(vx, -1, vx_rt) - vx) + (
            along_x(vy, -1, vy_dn) - vy
        )
        s[XX, z] += coef[C11, z] * xx + coef[C12, z] * yy + coef[C13, z] * zz
        s[YY, z] += coef[C12, z] * xx + coef[C22, z] * yy + coef[C23, z] * zz
        s[ZZ, z] += coef[C13, z] * xx + coef[C23, z] * yy + coef[C33, z] * zz
        s[YZ, z] += coef[C44, z] * yz
        s[XZ, z] += coef[C55, z] * xz
        s[XY, z] += coef[C66, z] * xy

    def velocity_layer(z, comps=(0, 1, 2)):
        is_bottom, is_top = isinstance(z, int) and z == bottom, isinstance(z, int) and z == top
        sxx, syy, szz = s[XX, z], s[YY, z], s[ZZ, z]
        syz, sxz, sxy = s[YZ, z], s[XZ, z], s[XY, z]
        b = coef[BUOY, z]
        if 0 in comps:
            v[0, z] += b * (
                (along_x(sxx, -1, halo_row[0, pl.ds(z, 1), :]) - sxx)
                + (sxy - along_y(sxy, 1, first_lane(halo_col.at[1], 0, z)))
                + (sxz if is_bottom else sxz - s[XZ, z - 1])
            )
        if 1 in comps:
            v[1, z] += b * (
                (sxy - along_x(sxy, 1, halo_row[1, pl.ds(z, 1), :]))
                + (along_y(syy, -1, last_lane(halo_col.at[0], 0, z)) - syy)
                + (syz if is_bottom else syz - s[YZ, z - 1])
            )
        if 2 in comps:
            v[2, z] += b * (
                (sxz - along_x(sxz, 1, halo_row[2, pl.ds(z, 1), :]))
                + (syz - along_y(syz, 1, first_lane(halo_col.at[2], 0, z)))
                + (-szz if is_top else s[ZZ, z + 1] - szz)
            )

    wide = (depth, size_y)
    wide_lane = iota(wide, 1)
    wide_z = iota(wide, 0)

    def below_z(f):
        return jnp.where(wide_z == 0, 0.0, pltpu.roll(f, 1, 0))

    def above_z(f):
        return jnp.where(wide_z == depth - 1, 0.0, pltpu.roll(f, depth - 1, 0))

    def lane_below_z(f):
        return jnp.where(lane == 0, 0.0, pltpu.roll(f, 1, 1))

    def lane_above_z(f):
        return jnp.where(lane == depth - 1, 0.0, pltpu.roll(f, LANES - 1, 1))

    def to_lanes(corner, at):
        col = jnp.broadcast_to(corner[:, at : at + 1], (depth, LANES))
        here = iota((depth, LANES), 0) == iota((depth, LANES), 1)
        return jnp.sum(jnp.where(here, col, 0.0), axis=0, keepdims=True)

    def lanes_of(ref, field):
        if field == 0:
            return ref[...]
        return pltpu.roll(ref[...], LANES - field * depth, 1)

    narrow_row = iota((size_x, LANES), 0)

    def halo_stress(up_ref, dn_ref, lt_ref, rt_ref, cup, cdn, my_up, my_dn, my_lt, my_rt):
        def rows(ref, k):
            return ref[k * depth : (k + 1) * depth, :]

        vx, vy, vz = rows(dn_ref, 0), rows(dn_ref, 1), rows(dn_ref, 2)
        corner = jnp.broadcast_to(cdn[:, LANES - 1 : LANES], wide)
        vy_back = jnp.where(wide_lane == 0, corner, pltpu.roll(vy, 1, 1))
        halo_row[0] += (
            hcoef_row[0] * (vx - rows(my_dn, 0))
            + hcoef_row[1] * (vy - vy_back)
            + hcoef_row[2] * (vz - below_z(vz))
        )
        vx, vy, vz = rows(up_ref, 0), rows(up_ref, 1), rows(up_ref, 2)
        corner = jnp.broadcast_to(cup[:, 0:1], wide)
        vx_next = jnp.where(wide_lane == size_y - 1, corner, pltpu.roll(vx, size_y - 1, 1))
        halo_row[1] += hcoef_row[3] * ((vx_next - vx) + (rows(my_up, 1) - vy))
        halo_row[2] += hcoef_row[4] * ((above_z(vx) - vx) + (rows(my_up, 2) - vz))
        vx, vy, vz = lanes_of(rt_ref, 0), lanes_of(rt_ref, 1), lanes_of(rt_ref, 2)
        vx_back = jnp.where(narrow_row == 0, to_lanes(cup, 0), pltpu.roll(vx, 1, 0))
        halo_col[0] += (
            hcoef_col[0] * (vx - vx_back)
            + hcoef_col[1] * (vy - lanes_of(my_rt, 1))
            + hcoef_col[2] * (vz - lane_below_z(vz))
        )
        vx, vy, vz = lanes_of(lt_ref, 0), lanes_of(lt_ref, 1), lanes_of(lt_ref, 2)
        vy_next = jnp.where(
            narrow_row == size_x - 1, to_lanes(cdn, LANES - 1), pltpu.roll(vy, size_x - 1, 0)
        )
        halo_col[1] += hcoef_col[3] * ((lanes_of(my_lt, 0) - vx) + (vy_next - vy))
        halo_col[2] += hcoef_col[4] * ((lane_above_z(vy) - vy) + (lanes_of(my_lt, 2) - vz))

    def stress_inside(z, _):
        stress_layer(z, None, None, None, None)
        return 0

    stress_inside(bottom, 0)
    lax.fori_loop(bottom + 1, top, stress_inside, 0)
    stress_inside(top, 0)

    wait_all(gathered, (n_p - 1) * per, group_recv, 0)
    rows = gathered[...]
    pick = taken[...].astype(BF16)
    routes = sum(dot(pick, part) for part in split(rows))
    early, late = routes[: n_z * 8], routes[n_z * 8 :]
    low_all = iota((n_z * 8, LANES), 1) < 64
    force0 = jnp.where(low_all, early, pltpu.roll(late, 64, 1))
    force1 = jnp.where(low_all, pltpu.roll(early, 64, 1), late)
    for k in range(n_z):
        send2[k, 0:8, :] = force0[k * 8 : (k + 1) * 8]
        send2[k, 8:16, :] = force1[k * 8 : (k + 1) * 8]
    for i in z_order:
        send(send2.at[xor(my_z, i)], routed2.at[my_z], z_partner(i), 1).start()
    routed2[my_z] = send2[my_z]

    at_x0 = aux_t[:, 1:2] == 0.0
    at_y0 = aux_t[:, 2:3] == 0.0
    along_row = jnp.where(at_x0, rows, pltpu.roll(rows, LANES - PATCH * reach, 1))
    along_col = jnp.where(at_y0, rows, pltpu.roll(rows, LANES - reach, 1))
    in_row = jnp.logical_and(off_y[...] >= 0, off_y[...] < PATCH)
    at = jnp.where(in_row, off_y[...], 0)
    parts = [
        jnp.take_along_axis(along_row, at[:, k : k + LANES], axis=1)
        for k in range(0, size_y, LANES)
    ]
    row_line = jnp.where(in_row, jnp.concatenate(parts, axis=1), 0.0)
    in_col = jnp.logical_and(off_x[...] >= 0, off_x[...] < PATCH)
    at = jnp.where(in_col, off_x[...] * PATCH, 0)
    col_line = jnp.where(in_col, jnp.take_along_axis(along_col, at, axis=1), 0.0)
    lines = jnp.concatenate([row_line, col_line], axis=1)
    pick = edge_pick[...].astype(BF16)
    lines = sum(dot(pick, part) for part in split(lines))
    send3[...] = jnp.where(
        side < 2, lines[:, :LANES], jnp.where(side < 4, lines[:, LANES:size_y], lines[:, size_y:])
    )
    for i in z_order:
        send(block(send3, xor(my_z, i), 8), block(routed3, my_z, 8), z_partner(i), 2).start()
    own = pl.ds(pl.multiple_of(my_z * 8, 8), 8)
    routed3[own, :] = send3[own, :]

    arrive1()
    kind = from_dn[4 * depth : 5 * depth, :]
    inside = has_dn.astype(F32)
    for k, index in enumerate((C11, C12, C13)):
        hcoef_row[k] = table(kind, index) * inside
    kind = from_up[5 * depth : 6 * depth, :]
    inside = has_up.astype(F32)
    for k, index in enumerate((C66, C55)):
        hcoef_row[3 + k] = table(kind, index) * inside
    kind = lanes_of(from_rt, 4)
    inside = has_rt.astype(F32)
    for k, index in enumerate((C12, C22, C23)):
        hcoef_col[k] = table(kind, index) * inside
    kind = lanes_of(from_lt, 5)
    inside = has_lt.astype(F32)
    for k, index in enumerate((C66, C44)):
        hcoef_col[3 + k] = table(kind, index) * inside
    halo_row[0] = from_dn[3 * depth : 4 * depth, :]
    halo_row[1] = from_up[3 * depth : 4 * depth, :]
    halo_row[2] = from_up[4 * depth : 5 * depth, :]
    halo_col[0] = lanes_of(from_rt, 3)
    halo_col[1] = lanes_of(from_lt, 3)
    halo_col[2] = lanes_of(from_lt, 4)

    def velocity_body(z, _):
        velocity_layer(z)
        return 0

    last_x = size_x - 1
    for z in range(depth):
        vx_up = from_up[z : z + 1, :]
        vy_dn, vz_dn = (from_dn[k * depth + z : k * depth + z + 1, :] for k in (1, 2))
        for comp, index in ((XX, C11), (YY, C12), (ZZ, C13)):
            s[comp, z, 0:1, :] -= coef[index, z, 0:1, :] * vx_up
        s[XZ, z, last_x:, :] += coef[C55, z, last_x:, :] * vz_dn
        s[XY, z, last_x:, :] += coef[C66, z, last_x:, :] * vy_dn
        vy_lt = jnp.where(lane == 0, first_lane(from_lt, 1, z), 0.0)
        for comp, index in ((XX, C12), (YY, C22), (ZZ, C23)):
            s[comp, z, :, :LANES] -= coef[index, z, :, :LANES] * vy_lt
        vx_rt, vz_rt = (
            jnp.where(lane == LANES - 1, last_lane(from_rt, k, z), 0.0) for k in (0, 2)
        )
        s[YZ, z, :, half:] += coef[C44, z, :, half:] * vz_rt
        s[XY, z, :, half:] += coef[C66, z, :, half:] * vx_rt
    halo_stress(
        from_up, from_dn, from_lt, from_rt, corner_up, corner_dn, to_up, to_dn, to_lt, to_rt
    )
    velocity_layer(bottom)
    lax.fori_loop(bottom + 1, top, velocity_body, 0)
    velocity_layer(top)

    pack_rows(vto_dn, size_x - 1, v_rows)
    pack_rows(vto_up, 0, v_rows)
    pack_cols(vto_rt, size_y - 1, v_cols)
    pack_cols(vto_lt, 0, v_cols)
    start2()

    def in_slot(t):
        return slot_x[t : t + 1, :] == x_ids

    wait_all(routed2, n_z - 1, group_recv, 1)
    force = routed2[0]
    for k in range(1, n_z):
        force = force + routed2[k]
    wide_force = jnp.concatenate(
        [
            jnp.concatenate(
                [jnp.where(in_slot(t), f[t : t + 1, :], 0.0) for t in range(8)], axis=1
            )
            for f in (force[0:8], force[8:16])
        ],
        axis=0,
    )
    got = dot(jnp.concatenate(split(wide_force), axis=0), onehot_y[...], ((1,), (1,)))
    got = got[: 2 * size_x] + got[2 * size_x :]
    plane[...] = coef[BUOY, top] * got[size_x:]
    top0 = v[2, top] + coef[BUOY, top] * got[:size_x]
    v[2, top] = top0

    def sample(values, step):
        got = dot(jnp.concatenate(split(values), axis=0), onehot_y[...])
        got = got[:size_x] + got[size_x:]
        for t in range(8):
            chosen = jnp.where(in_slot(t), got[:, t * LANES : (t + 1) * LANES], 0.0)
            at = step * 8 + t
            rec_send[at : at + 1, :] = jnp.sum(chosen, axis=0, keepdims=True)

    sample(top0, 0)
    wait_all(routed3, (n_z - 1) * 8, group_recv, 2)
    lines = routed3[0:8, :]
    for k in range(1, n_z):
        lines = lines + routed3[k * 8 : (k + 1) * 8, :]
    top_row = 2 * depth + top
    arrive2()
    leave2()

    def buoyancy(kind):
        return table(kind, BUOY)

    wide_line = jnp.concatenate([lines[0:2], lines[2:4]], axis=1)
    kind = from_dn[4 * depth + top : 4 * depth + top + 1, :]
    vfrom_dn[top_row : top_row + 1, :] += buoyancy(kind) * wide_line[0:1]
    kind = from_up[5 * depth + top : 5 * depth + top + 1, :]
    vfrom_up[top_row : top_row + 1, :] += buoyancy(kind) * wide_line[1:2]
    diagonal = iota((size_x, LANES), 0) == lane

    def upright(line):
        return jnp.sum(jnp.where(diagonal, line, 0.0), axis=1, keepdims=True)

    kind = pltpu.roll(from_rt[...], (top_row - 4 * depth - top) % LANES, 1)
    vfrom_rt[...] += jnp.where(lane == top_row, buoyancy(kind) * upright(lines[4:5]), 0.0)
    kind = pltpu.roll(from_lt[...], (top_row - 5 * depth - top) % LANES, 1)
    vfrom_lt[...] += jnp.where(lane == top_row, buoyancy(kind) * upright(lines[5:6]), 0.0)
    vto_up[top_row : top_row + 1, :] = v[2, top, 0:1, :]
    vto_lt[...] = jnp.where(
        lane == top_row, pltpu.roll(v[2, top, :, :LANES], top_row, 1), vto_lt[...]
    )
    stress_layer(top, vfrom_up, vfrom_dn, vfrom_lt, vfrom_rt)
    halo_stress(
        vfrom_up,
        vfrom_dn,
        vfrom_lt,
        vfrom_rt,
        vcorner_up,
        vcorner_dn,
        vto_up,
        vto_dn,
        vto_lt,
        vto_rt,
    )
    velocity_layer(top, (2,))
    top1 = v[2, top] + plane[...]
    v[2, top] = top1

    sample(top1, 1)
    for i in z_order:
        send(rec_send, rec_rows.at[my_z], z_partner(i), 3).start()
    rec_rows[my_z] = rec_send[...]

    pick = taken_t[...].astype(BF16)
    wait_all(rec_rows, n_z - 1, group_recv, 3)
    early = rec_rows[:, 0:8, :].reshape(n_z * 8, LANES)
    late = rec_rows[:, 8:16, :].reshape(n_z * 8, LANES)
    both = jnp.concatenate(
        [
            jnp.where(low_all, early, pltpu.roll(late, 64, 1)),
            jnp.where(low_all, pltpu.roll(early, 64, 1), late),
        ],
        axis=0,
    )
    back = sum(dot(pick, part) for part in split(both))
    rec_back[...] = back
    for i in p_order:
        send(block(rec_back, xor(my_p, i), per), block(rec_got, my_p, per), p_partner(i), 4).start()
    mine = pl.ds(pl.multiple_of(my_p * per, per), per)
    rec_got[mine, :] = rec_back[mine, :]
    def stress_second(z, _):
        stress_layer(z, vfrom_up, vfrom_dn, vfrom_lt, vfrom_rt)
        return 0

    stress_second(bottom, 0)
    lax.fori_loop(bottom + 1, top, stress_second, 0)
    velocity_layer(bottom)
    lax.fori_loop(bottom + 1, top, velocity_body, 0)
    velocity_layer(top, (0, 1))

    leave1()
    wait_all(gathered, (n_p - 1) * per, group_send, 0)
    wait_all(routed2, n_z - 1, group_send, 1)
    wait_all(routed3, (n_z - 1) * 8, group_send, 2)
    wait_all(rec_rows, n_z - 1, group_send, 3)
    wait_all(rec_got, (n_p - 1) * per, group_recv, 4)
    tile = max(per, 8)
    parts = [rec_got[i * tile : (i + 1) * tile, :] for i in range(n_p * per // tile)]
    while len(parts) > 1:
        parts = [a + b for a, b in zip(parts[::2], parts[1::2])]
    out = parts[0][:per]
    for i in range(1, tile // per):
        out = out + parts[0][i * per : (i + 1) * per]
    rec_out[...] = out

    wait_all(rec_got, (n_p - 1) * per, group_send, 4)


def hand_over(v, s, rec, vel_out, str_out, rec_out, sem):
    pairs = [(v, vel_out), (s, str_out), (rec, rec_out)]
    copies = [pltpu.make_async_copy(a, b, sem.at[i]) for i, (a, b) in enumerate(pairs)]
    for copy in copies:
        copy.start()
    for copy in copies:
        copy.wait()


def solution(mesh):
    n_chord, n_span = mesh.shape["chord"], mesh.shape["span"]

    def local(velocity, stress, material, moduli, drive, owner, cells):
        _, depth, size_x, size_y = velocity.shape
        per = drive.shape[0]

        def mem(*shape):
            return pltpu.VMEM(shape, F32)

        def edges(rows_dn, rows_up):
            return [
                mem(rows_dn * depth, size_y),
                mem(rows_up * depth, size_y),
                mem(size_x, LANES),
                mem(size_x, LANES),
            ]

        layer = (size_x, size_y)
        vmem = pl.BlockSpec(memory_space=pltpu.VMEM)
        slots = SPLIT_Z * SLOTS
        n_p = n_chord * SPLIT_X_HI * SPLIT_CORE
        inputs = (velocity, stress, material, moduli, drive, owner.reshape(-1, LANES), cells.T)
        state = pl.pallas_call(
            functools.partial(kernel, n_chord, n_span),
            out_shape=(
                jax.ShapeDtypeStruct(velocity.shape, F32),
                jax.ShapeDtypeStruct(stress.shape, F32),
                jax.ShapeDtypeStruct(drive.shape, F32),
            ),
            in_specs=[pl.BlockSpec(memory_space=pltpu.HBM)] * 7,
            out_specs=(vmem, vmem, vmem),
            scratch_shapes=[
                pltpu.VMEM((depth, *layer), jnp.int32),
                pltpu.SMEM(moduli.shape, F32),
                mem(*drive.shape),
                pltpu.VMEM((owner.size // LANES, LANES), jnp.int32),
                pltpu.VMEM((8, owner.size), jnp.int32),
                mem(10, depth, *layer),
                pltpu.VMEM((size_y, 8 * LANES), BF16),
                mem(8, LANES),
                mem(8, LANES),
                mem(*layer),
                mem(owner.size // LANES * SPLIT_Z, LANES),
                mem(slots, LANES),
                mem(LANES, slots),
                mem(n_p * per, LANES),
                mem(SPLIT_Z, 16, LANES),
                mem(SPLIT_Z, 16, LANES),
                mem(slots // 2, LANES),
                mem(slots // 2, LANES),
                mem(SLOTS, LANES),
                mem(SPLIT_Z, SLOTS, LANES),
                mem(n_p * per, LANES),
                mem(n_p * per, LANES),
                *edges(6, 5),
                mem(6 * depth, size_y),
                mem(5 * depth, size_y),
                mem(size_x, LANES),
                mem(size_x, LANES),
                mem(depth, LANES),
                mem(depth, LANES),
                *edges(3, 3),
                *edges(3, 3),
                mem(depth, LANES),
                mem(depth, LANES),
                mem(LANES, LANES),
                pltpu.VMEM((LANES, size_y), jnp.int32),
                pltpu.VMEM((LANES, LANES), jnp.int32),
                mem(SPLIT_Z * 8, LANES),
                mem(3, depth, size_y),
                mem(3, size_x, LANES),
                mem(5, depth, size_y),
                mem(5, size_x, LANES),
                pltpu.SemaphoreType.DMA((7,)),
                pltpu.SemaphoreType.DMA((5,)),
                pltpu.SemaphoreType.DMA((5,)),
                pltpu.SemaphoreType.DMA((12,)),
                pltpu.SemaphoreType.DMA((12,)),
            ],
            compiler_params=pltpu.CompilerParams(
                collective_id=0, has_side_effects=True, vmem_limit_bytes=48 * 1024 * 1024
            ),
        )(*(pltpu.with_memory_space_constraint(x, pltpu.HBM) for x in inputs))
        hbm = pl.BlockSpec(memory_space=pltpu.HBM)
        return pl.pallas_call(
            hand_over,
            out_shape=tuple(jax.ShapeDtypeStruct(x.shape, x.dtype) for x in state),
            in_specs=[pl.BlockSpec(memory_space=pl.ANY)] * 3,
            out_specs=(hbm, hbm, hbm),
            scratch_shapes=[pltpu.SemaphoreType.DMA((3,))],
        )(*(pltpu.with_memory_space_constraint(x, pltpu.VMEM) for x in state))

    in_specs = (
        P(None, None, "chord", "span"),
        P(None, None, "chord", "span"),
        P(None, "chord", "span"),
        P(),
        P(("chord", "span"), None),
        P(),
        P(),
    )
    out_specs = (
        P(None, None, "chord", "span"),
        P(None, None, "chord", "span"),
        P(("chord", "span"), None),
    )
    return jax.shard_map(local, mesh=mesh, in_specs=in_specs, out_specs=out_specs, check_vma=False)
```

profile of v0, /device:TPU:1, one launch (start us, length us, event | category | flops | bytes accessed | tf_op | source)
XLA Modules:
  0.0 33.6 jit_solution(1010140764166984477)
XLA Ops:
  0.6 31.6 %shard_map.94 = (f32[3,8,32,256]{3,2,1,0:T(8,128)S(1)}, f32[6,8,32,256]{3,2,1,0:T(8,128)S(1)}, f32[4,128]{1,0:T(4,128)S(1)}) custom-call(f32[3,8,32,256]{3,2,1,0:T(8,128)} %vel_in.1, f32[6,8,32,256]{3,2,1,0:T(8,128)} %str_in.1, s32[8,32,256]{2,1,0:T(8,128)} %mat_in.1, f32[4,10]{1,0:T(4,128)} %moduli_in.1, f32[4,128]{1,0:T(4,128)} %drive_in.1, ...), custom_call_target="tpu_custom_call" | custom-call | tf_op jit(solution)/shard_map/pallas_call | solution.py:828
  32.2 1.4 %shard_map.95 = (f32[3,8,32,256]{3,2,1,0:T(8,128)}, f32[6,8,32,256]{3,2,1,0:T(8,128)}, f32[4,128]{1,0:T(4,128)}) custom-call(f32[3,8,32,256]{3,2,1,0:T(8,128)S(1)} %get-tuple-element.6.v, f32[6,8,32,256]{3,2,1,0:T(8,128)S(1)} %get-tuple-element.7.s, f32[4,128]{1,0:T(4,128)S(1)} %get-tuple-element.8.rec), custom_call_target="tpu_custom_call" | custom-call | tf_op jit(solution)/shard_map/pallas_call | solution.py:890
where the time goes:
time: 33.7 us; the launch traced here: 33.6 us
  Pallas kernels  33 us (98%)
  between operations  0.64 us (2%)
    pallas_call x1, Pallas kernels, local(): pl.pallas_call(functools.partial(kernel, n_chord, n_span), out_shape=(jax...  31.6 us
    pallas_call x1, Pallas kernels, local(): pl.pallas_call(hand_over, out_shape=tuple((jax.ShapeDtypeStruct(x.shape,...  1.43 us

commit v1 on v0

--- a/solution.py
+++ b/solution.py
@@ -61,7 +61,9 @@
     plane,
     ranks,
     taken,
-    taken_t,
+    pick_out,
+    pick_back,
+    pick_edge,
     gathered,
     send2,
     routed2,
@@ -160,8 +162,6 @@
     for i in z_order:
         greet(*z_partner(i))
     sides = [
-        (has_up, (c - 1, sp)),
-        (has_dn, (c + 1, sp)),
         (has_lt, (c, sp - 1)),
         (has_rt, (c, sp + 1)),
         (diag_up, (c - 1, sp + 1)),
@@ -394,7 +394,9 @@
     off_x[...] = iota((LANES, LANES), 1) - aux_t[:, 1:2].astype(jnp.int32)
     off_y[...] = iota((LANES, size_y), 1) - aux_t[:, 2:3].astype(jnp.int32)
 
-    taken_t[...] = jnp.transpose(taken[...])
+    pick_out[...] = taken[...].astype(BF16)
+    pick_back[...] = jnp.transpose(taken[...]).astype(BF16)
+    pick_edge[...] = edge_pick[...].astype(BF16)
     first_x = jnp.zeros((SLOTS, LANES), F32)
     first_y = jnp.zeros((SLOTS, LANES), F32)
     for a in range(n_block):
@@ -571,7 +573,7 @@
 
     wait_all(gathered, (n_p - 1) * per, group_recv, 0)
     rows = gathered[...]
-    pick = taken[...].astype(BF16)
+    pick = pick_out[...]
     routes = sum(dot(pick, part) for part in split(rows))
     early, late = routes[: n_z * 8], routes[n_z * 8 :]
     low_all = iota((n_z * 8, LANES), 1) < 64
@@ -599,7 +601,7 @@
     at = jnp.where(in_col, off_x[...] * PATCH, 0)
     col_line = jnp.where(in_col, jnp.take_along_axis(along_col, at, axis=1), 0.0)
     lines = jnp.concatenate([row_line, col_line], axis=1)
-    pick = edge_pick[...].astype(BF16)
+    pick = pick_edge[...]
     lines = sum(dot(pick, part) for part in split(lines))
     send3[...] = jnp.where(
         side < 2, lines[:, :LANES], jnp.where(side < 4, lines[:, LANES:size_y], lines[:, size_y:])
@@ -748,7 +750,7 @@
         send(rec_send, rec_rows.at[my_z], z_partner(i), 3).start()
     rec_rows[my_z] = rec_send[...]
 
-    pick = taken_t[...].astype(BF16)
+    pick = pick_back[...]
     wait_all(rec_rows, n_z - 1, group_recv, 3)
     early = rec_rows[:, 0:8, :].reshape(n_z * 8, LANES)
     late = rec_rows[:, 8:16, :].reshape(n_z * 8, LANES)
@@ -847,7 +849,9 @@
                 mem(*layer),
                 mem(owner.size // LANES * SPLIT_Z, LANES),
                 mem(slots, LANES),
-                mem(LANES, slots),
+                pltpu.VMEM((slots, LANES), BF16),
+                pltpu.VMEM((LANES, slots), BF16),
+                pltpu.VMEM((slots // 2, LANES), BF16),
                 mem(n_p * per, LANES),
                 mem(SPLIT_Z, 16, LANES),
                 mem(SPLIT_Z, 16, LANES),

time: 33.7 us -> 33.7 us (level)
  no operation moved by 1% of the time
where the time goes in v1:
time: 33.7 us; the launch traced here: 33.6 us
  Pallas kernels  33 us (98%)
  between operations  0.64 us (2%)
    pallas_call x1, Pallas kernels, local(): pl.pallas_call(functools.partial(kernel, n_chord, n_span), out_shape=(jax...  31.6 us
    pallas_call x1, Pallas kernels, local(): pl.pallas_call(hand_over, out_shape=tuple((jax.ShapeDtypeStruct(x.shape,...  1.43 us

profile of v1, /device:TPU:1, one launch (start us, length us, event | category | flops | bytes accessed | tf_op | source)
XLA Modules:
  0.0 33.6 jit_solution(15575917616699942549)
XLA Ops:
  0.6 31.6 %shard_map.94 = (f32[3,8,32,256]{3,2,1,0:T(8,128)S(1)}, f32[6,8,32,256]{3,2,1,0:T(8,128)S(1)}, f32[4,128]{1,0:T(4,128)S(1)}) custom-call(f32[3,8,32,256]{3,2,1,0:T(8,128)} %vel_in.1, f32[6,8,32,256]{3,2,1,0:T(8,128)} %str_in.1, s32[8,32,256]{2,1,0:T(8,128)} %mat_in.1, f32[4,10]{1,0:T(4,128)} %moduli_in.1, f32[4,128]{1,0:T(4,128)} %drive_in.1, ...), custom_call_target="tpu_custom_call" | custom-call | tf_op jit(solution)/shard_map/pallas_call | solution.py:830
  32.2 1.4 %shard_map.95 = (f32[3,8,32,256]{3,2,1,0:T(8,128)}, f32[6,8,32,256]{3,2,1,0:T(8,128)}, f32[4,128]{1,0:T(4,128)}) custom-call(f32[3,8,32,256]{3,2,1,0:T(8,128)S(1)} %get-tuple-element.6.v, f32[6,8,32,256]{3,2,1,0:T(8,128)S(1)} %get-tuple-element.7.s, f32[4,128]{1,0:T(4,128)S(1)} %get-tuple-element.8.rec), custom_call_target="tpu_custom_call" | custom-call | tf_op jit(solution)/shard_map/pallas_call | solution.py:894
